TPU v7x, 128 devices: a whole 4x4x4 slice. The times are simulated.
128 devices in a mesh: ctx: 8 (over y, core), batch: 16 (over x, z).
Axes of the slice: x: 4, y: 4, z: 4, core: 2. Of those that a mesh axis runs over, the one named last changes fastest.
Arguments:
- queries: bfloat16 [512, 8192], P('batch'), may hold values from -200 to 200
- seq_doc: int32 [512, 1], P('batch'), may hold values from 0 to 3; in each aligned block of 32 rows (0 to 31, 32 to 63, ...) at most 16 rows name the same one
- suffix_lengths: int32 [512], P('batch'), may hold values from 1 to 32, as said below
- prefix_keys: bfloat16 [16, 8192, 1024], P('batch', 'ctx'), may hold values from -6 to 6
- prefix_values: bfloat16 [16, 8192, 1024], P('batch', 'ctx'), may hold values from -6 to 6
- suffix_keys: bfloat16 [512, 32, 1024], P('batch'), may hold values from -9 to 9
- suffix_values: bfloat16 [512, 32, 1024], P('batch'), may hold values from -6 to 6
Outputs:
- attended: bfloat16 [512, 8192], P('batch')
Inputs may be any that keep to these rules, and one draw needn't show every extreme that they name: `seq_doc`: among the rows of one index of batch, no document is read by more than 16 sequences. Sequence r's private suffix holds the first suffix_lengths[r] positions of its cache.
All inputs are finite; a program needn't handle non-finite values.
Results may differ from a plain program's by a relative error of at most 0.014.
Values may be sent and summed in bfloat16 or wider, within the bound.
A program may use at most 192 MiB of HBM per device.

v0:
```python
from functools import reduce

import jax
import jax.numpy as jnp
from jax import lax
from jax.sharding import PartitionSpec as P

H = 64
KVH = 8
HD = 128
DOCS = 4
MOST = 16


def combined_all(part, axis, combine):
    gathered = jax.tree.map(lambda a: lax.all_gather(a, axis), part)

    def take(source):
        return jax.tree.map(lambda a: lax.dynamic_index_in_dim(a, source, 0, False), gathered)

    return lax.fori_loop(
        1, lax.axis_size(axis), lambda source, state: combine(state, take(source)), take(0)
    )


def local_partial(query_rows, doc_keys, doc_values):
    row_count = query_rows.shape[0]
    positions = doc_keys.shape[0]
    query_heads = query_rows.reshape(row_count, KVH, H // KVH, HD)
    key_heads = doc_keys.reshape(positions, KVH, HD)
    value_heads = doc_values.reshape(positions, KVH, HD)
    scores = jnp.einsum(
        "rkgd,pkd->rkgp", query_heads, key_heads, preferred_element_type=jnp.float32
    ) * HD ** (-0.5)
    row_max = jnp.max(scores, axis=-1)
    weights = jnp.exp(scores - row_max[..., None])
    totals = jnp.sum(weights, axis=-1)
    attended = jnp.einsum(
        "rkgp,pkd->rkgd",
        weights.astype(jnp.bfloat16),
        value_heads,
        preferred_element_type=jnp.float32,
    )
    return (
        row_max.reshape(row_count, H),
        totals.reshape(row_count, H),
        attended.reshape(row_count, H, HD),
    )


def suffix_part(queries, suffix_keys, suffix_values, suffix_lengths):
    row_count = suffix_keys.shape[0]
    cache_size = suffix_keys.shape[1]
    query_heads = queries.reshape(row_count, KVH, H // KVH, HD)
    key_heads = suffix_keys.reshape(row_count, cache_size, KVH, HD)
    value_heads = suffix_values.reshape(row_count, cache_size, KVH, HD)
    scores = jnp.einsum(
        "rkgd,rtkd->rkgt", query_heads, key_heads, preferred_element_type=jnp.float32
    ) * HD ** (-0.5)
    in_cache = (jnp.arange(cache_size, dtype=jnp.int32)[None, :] < suffix_lengths[:, None])[
        :, None, None, :
    ]
    scores = jnp.where(in_cache, scores, -jnp.inf)
    row_max = jnp.max(scores, axis=-1)
    weights = jnp.where(in_cache, jnp.exp(scores - row_max[..., None]), 0.0)
    totals = jnp.sum(weights, axis=-1)
    attended = jnp.einsum(
        "rkgt,rtkd->rkgd",
        weights.astype(jnp.bfloat16),
        value_heads,
        preferred_element_type=jnp.float32,
    )
    return (
        row_max.reshape(row_count, H),
        totals.reshape(row_count, H),
        attended.reshape(row_count, H, HD),
    )


def combine_parts(earlier_part, later_part):
    maxima = jnp.maximum(earlier_part[0], later_part[0])
    left_scale = jnp.exp(earlier_part[0] - maxima)
    right_scale = jnp.exp(later_part[0] - maxima)
    totals = earlier_part[1] * left_scale + later_part[1] * right_scale
    attended = earlier_part[2] * left_scale[..., None] + later_part[2] * right_scale[..., None]
    return (maxima, totals, attended)


def on_device(
    queries, seq_doc, suffix_lengths, prefix_keys, prefix_values, suffix_keys, suffix_values
):
    row_count = queries.shape[0]
    feature_width = queries.shape[1]
    doc_ids = seq_doc[:, 0]
    devices = lax.axis_size("batch")
    group_size = devices // DOCS
    capacity = MOST
    onehot = (doc_ids[:, None] == jnp.arange(DOCS, dtype=jnp.int32)[None, :]).astype(jnp.int32)
    earlier = jnp.cumsum(onehot, axis=0) - onehot
    ranking = jnp.sum(earlier * onehot, axis=1)
    by_doc = (
        jnp.zeros((DOCS, capacity, feature_width), queries.dtype).at[doc_ids, ranking].set(queries)
    )
    outgoing = jnp.repeat(by_doc, group_size, axis=0)
    block_keys = prefix_keys[0]
    block_values = prefix_values[0]
    arrived = lax.all_to_all(outgoing, "batch", split_axis=0, concat_axis=0, tiled=True)
    sources, slot_count, width = arrived.shape
    row_max, totals, attended = local_partial(
        arrived.reshape(sources * slot_count, width), block_keys, block_values
    )
    returned_parts = (
        lax.all_to_all(
            row_max.reshape(sources, slot_count, H),
            "batch",
            split_axis=0,
            concat_axis=0,
            tiled=True,
        ),
        lax.all_to_all(
            totals.reshape(sources, slot_count, H), "batch", split_axis=0, concat_axis=0, tiled=True
        ),
        lax.all_to_all(
            attended.reshape(sources, slot_count, H, HD),
            "batch",
            split_axis=0,
            concat_axis=0,
            tiled=True,
        ),
    )
    picked = tuple(
        (
            member.reshape((DOCS, group_size, capacity) + member.shape[2:])[doc_ids, :, ranking]
            for member in returned_parts
        )
    )
    prefix = reduce(
        combine_parts,
        [tuple((member[:, block] for member in picked)) for block in range(group_size)],
    )
    suffix_stats = suffix_part(queries, suffix_keys, suffix_values, suffix_lengths)
    merged = combined_all(prefix, "ctx", combine_parts)
    combined = combine_parts(merged, suffix_stats)
    result = (combined[2] / combined[1][..., None]).astype(jnp.bfloat16).reshape(row_count, H * HD)
    return result


def solution(mesh):
    in_specs = (
        P("batch", None),
        P("batch", None),
        P("batch"),
        P("batch", "ctx", None),
        P("batch", "ctx", None),
        P("batch", None, None),
        P("batch", None, None),
    )
    out_specs = P("batch", None)
    return jax.shard_map(
        on_device, mesh=mesh, in_specs=in_specs, out_specs=out_specs, check_vma=False
    )
```

profile of v0, /device:TPU:1, one launch (start us, length us, event | category | flops | bytes accessed | tf_op | source)
XLA Modules:
  0.0 441.5 jit_solution(11394536917586915375)
XLA Ops:
  6.5 0.9 fusion.71
  7.5 0.8 select_reduce_fusion
  9.0 12.2 %scatter_fusion = bf16[4,16,8192]{2,1,0:T(8,128)(2,1)S(1)} fusion(bf16[4,16,8192]{2,1,0:T(8,128)(2,1)S(1)} %broadcast_in_dim.22, s32[32]{0:T(128)S(1)} %get-tuple-element.209, bf16[32,8192]{1,0:T(8,128)(2,1)} %param.9), kind=kCustom, calls=%fused_computation.3 | custom fusion | bytes 1573120 | tf_op jit(solution)/shard_map/scatter | solution.py:102
  21.2 2.4 broadcast_in_dim.23
  23.7 8.5 %all-to-all-start = ((bf16[16,16,8192]{2,1,0:T(8,128)(2,1)}), bf16[16,16,8192]{2,1,0:T(8,128)(2,1)}, u32[]{:S(2)}, u32[]{:S(2)}) async-start(bf16[16,16,8192]{2,1,0:T(8,128)(2,1)} %bitcast.268), calls=%async_computation | async-start | bytes 8388608 | tf_op jit(solution)/shard_map/all_to_all | solution.py:107
  32.2 3.7 copy.136
  35.9 2.0 copy.137
  37.9 55.8 %all-to-all-done = bf16[16,16,8192]{2,1,0:T(8,128)(2,1)} async-done(((bf16[16,16,8192]{2,1,0:T(8,128)(2,1)}), bf16[16,16,8192]{2,1,0:T(8,128)(2,1)}, u32[]{:S(2)}, u32[]{:S(2)}) %all-to-all-start) | async-done | bytes 4194336 | tf_op jit(solution)/shard_map/all_to_all | solution.py:107
  93.7 5.4 %copy.135 = bf16[32,8,64,128]{3,2,1,0:T(8,128)(2,1)} copy(bf16[32,8,64,128]{3,1,2,0:T(8,128)(2,1)} %bitcast.67) | data formatting | bytes 8388608
  99.0 35.2 %bitcast_reduce_fusion = (f32[256,8,8]{0,2,1:T(8,128)S(1)}, f32[8,256,8,1024]{3,1,2,0:T(8,128)}) fusion(bf16[1024,8,128,1]{2,1,0,3:T(8,128)(2,1)} %bitcast.271, bf16[256,8,8,128]{3,2,1,0:T(8,128)(2,1)} %bitcast.269), kind=kOutput, calls=%fused_computation.13 | convolution fusion | flops 4328505344 | bytes 73465856 | tf_op jit(solution)/shard_map/rkgd,pkd->rkgp/dot_general | solution.py:32
  134.6 0.8 reshape.415
  135.4 9.7 %all-to-all-start.1 = ((f32[16,1,1024]{2,1,0:T(1,128)}), f32[16,1,1024]{2,1,0:T(1,128)S(1)}, u32[]{:S(2)}, u32[]{:S(2)}) async-start(f32[16,1,1024]{2,1,0:T(1,128)} %reshape.415), calls=%async_computation.1 | async-start | bytes 131072 | tf_op jit(solution)/shard_map/all_to_all | solution.py:113
  145.1 27.6 %fusion.6 = f32[8,256,8,128]{3,1,2,0:T(8,128)} fusion(f32[8,256,8,1024]{3,1,2,0:T(8,128)} %get-tuple-element.227, f32[256,8,8]{0,2,1:T(8,128)S(1)} %get-tuple-element.226, bf16[1024,8,128,1]{2,1,0,3:T(8,128)(2,1)} %bitcast.270), kind=kOutput, calls=%fused_computation.17 | convolution fusion | flops 4345298944 | bytes 77660160 | tf_op jit(solution)/shard_map/rkgp,pkd->rkgd/dot_general | solution.py:38
  172.7 7.6 %copy.105 = f32[16,16,64,128]{3,1,2,0:T(8,128)} copy(f32[16,16,64,128]{3,1,0,2:T(8,128)} %bitcast.266) | data formatting | bytes 16777216 | tf_op jit(solution)/shard_map/reshape;reshape | solution.py:124
  180.3 6.7 %all-to-all-start.3 = ((f32[16,16,64,128]{3,1,2,0:T(8,128)}), f32[16,16,64,128]{3,1,2,0:T(8,128)}, u32[]{:S(2)}, u32[]{:S(2)}) async-start(f32[16,16,64,128]{3,1,2,0:T(8,128)} %copy.105), calls=%async_computation.3 | async-start | bytes 16777216 | tf_op jit(solution)/shard_map/all_to_all | solution.py:123
  187.6 0.8 reduce.1
  189.3 121.6 %all-to-all-done.3 = f32[16,16,64,128]{3,1,2,0:T(8,128)} async-done(((f32[16,16,64,128]{3,1,2,0:T(8,128)}), f32[16,16,64,128]{3,1,2,0:T(8,128)}, u32[]{:S(2)}, u32[]{:S(2)}) %all-to-all-start.3) | async-done | bytes 8388640 | tf_op jit(solution)/shard_map/all_to_all | solution.py:123
  310.9 9.3 %copy.106 = f32[16,16,64,128]{3,2,1,0:T(8,128)} copy(f32[16,16,64,128]{3,1,2,0:T(8,128)} %all-to-all-done.3) | data formatting | bytes 16777216 | tf_op jit(solution)/shard_map/all_to_all | solution.py:123
  320.2 6.2 %gather_fusion.2 = f32[32,4,64,128]{3,2,1,0:T(8,128)} fusion(f32[4,4,16,64,128]{4,3,2,1,0:T(8,128)} %bitcast.267, s32[32]{0:T(128)S(1)} %bitcast.273), kind=kCustom, calls=%fused_computation.2 | custom fusion | bytes 8388864 | tf_op jit(solution)/shard_map/gather | solution.py:133
  326.4 4.9 %fusion.42 = f32[1,32,64,128]{3,2,1,0:T(8,128)} fusion(f32[32,4,64,128]{3,2,1,0:T(8,128)} %gather_fusion.2, f32[32,64]{1,0:T(8,128)S(1)} %get-tuple-element.222, f32[32,64]{1,0:T(8,128)S(1)} %get-tuple-element.221, f32[32,64]{1,0:T(8,128)S(1)} %get-tuple-element.224, f32[32,64]{1,0:T(8,128)S(1)} %get-tuple-element.223, f32[32,64]{1,0:T(8,128)S(1)} %get-tuple-element.225, ...), kind=kLoop, calls=%fused_computation.40 | loop fusion | flops 2359296 | bytes 5292032 | tf_op jit(solution)/shard_map/add | solution.py:85
  331.5 2.9 fusion.82
  334.4 23.2 %fusion.5 = f32[256,8,8]{0,2,1:T(8,128)S(1)} fusion(f32[8,256,8,1024]{3,1,2,0:T(8,128)} %get-tuple-element.227, f32[256,8,8]{0,2,1:T(8,128)S(1)} %get-tuple-element.226), kind=kLoop, calls=%fused_computation.16 | loop fusion | flops 50315264 | bytes 67239936 | tf_op jit(solution)/shard_map/reduce_sum | solution.py:37
  357.6 1.0 reshape_reshape.14
  358.6 1.3 copy.98
  359.9 0.8 reshape.417
  360.6 7.4 %all-to-all-start.2 = ((f32[16,1,1024]{2,1,0:T(1,128)}), f32[16,1,1024]{2,1,0:T(1,128)S(1)}, u32[]{:S(2)}, u32[]{:S(2)}) async-start(f32[16,1,1024]{2,1,0:T(1,128)} %reshape.417), calls=%async_computation.2 | async-start | bytes 131072 | tf_op jit(solution)/shard_map/all_to_all | solution.py:120
  370.2 4.3 all-to-all-done.2
  374.5 0.8 reduce
  376.2 19.5 %all_gather.12 = f32[8,32,64]{2,1,0:T(8,128)S(1)} all-gather(f32[1,32,64]{2,1,0:T(8,128)S(1)} %get-tuple-element.212), channel_id=1, replica_groups=mesh['ctx'=8,'batch'=16] {'ctx'}, dimensions={0}, use_global_device_ids=true | all-gather | bytes 73728 | tf_op jit(solution)/shard_map/all_gather | solution.py:16
  395.7 12.7 %all_gather.13 = f32[8,32,64]{2,1,0:T(8,128)S(1)} all-gather(f32[1,32,64]{2,1,0:T(8,128)S(1)} %get-tuple-element.211), channel_id=1, replica_groups=mesh['ctx'=8,'batch'=16] {'ctx'}, dimensions={0}, use_global_device_ids=true | all-gather | bytes 73728 | tf_op jit(solution)/shard_map/all_gather | solution.py:16
  409.1 1.3 slice_bitcast_fusion
  410.4 20.7 %while.19 = (s32[]{:T(128)}, f32[32,64]{1,0:T(8,128)S(1)}, f32[32,64]{1,0:T(8,128)S(1)}, f32[32,64,128]{2,1,0:T(8,128)S(1)}, f32[8,32,64]{2,1,0:T(8,128)S(1)}, /...) while((s32[]{:T(128)}, f32[32,64]{1,0:T(8,128)S(1)}, ...), condition=%wide.region_6.7_spmd, body=%wide.region_5.6_spmd.sunk | while | flops 798725 | bytes 3227799 | solution.py:21
  410.4 0.7 fusion.88
  411.2 2.2 fusion.89
  413.4 0.7 fusion.88
  414.1 2.2 fusion.89
  416.3 0.7 fusion.88
  417.1 2.2 fusion.89
  419.3 0.7 fusion.88
  420.0 2.2 fusion.89
  422.2 0.7 fusion.88
  423.0 2.2 fusion.89
  425.2 0.7 fusion.88
  425.9 2.2 fusion.89
  428.2 0.7 fusion.88
  428.9 2.2 fusion.89
  431.2 2.3 fusion.38
  433.5 1.1 copy.175
  (47 shorter events, 6.7 us)
Async XLA Ops:
  6.5 424.6 %copy-start = (bf16[32,32,1024]{2,1,0:T(8,128)(2,1)S(1)}, bf16[32,32,1024]{2,1,0:T(8,128)(2,1)}, u32[]{:S(2)}) copy-start(bf16[32,32,1024]{2,1,0:T(8,128)(2,1)} %param.15) | copy-start | bytes 6291460
  23.7 70.0 %all-to-all-start = ((bf16[16,16,8192]{2,1,0:T(8,128)(2,1)}), bf16[16,16,8192]{2,1,0:T(8,128)(2,1)}, u32[]{:S(2)}, u32[]{:S(2)}) async-start(bf16[16,16,8192]{2,1,0:T(8,128)(2,1)} %bitcast.268), calls=%async_computation | async-start | bytes 8388608 | tf_op jit(solution)/shard_map/all_to_all | solution.py:107
  32.2 3.7 copy-start.3
  135.4 44.9 %all-to-all-start.1 = ((f32[16,1,1024]{2,1,0:T(1,128)}), f32[16,1,1024]{2,1,0:T(1,128)S(1)}, u32[]{:S(2)}, u32[]{:S(2)}) async-start(f32[16,1,1024]{2,1,0:T(1,128)} %reshape.415), calls=%async_computation.1 | async-start | bytes 131072 | tf_op jit(solution)/shard_map/all_to_all | solution.py:113
  180.3 130.6 %all-to-all-start.3 = ((f32[16,16,64,128]{3,1,2,0:T(8,128)}), f32[16,16,64,128]{3,1,2,0:T(8,128)}, u32[]{:S(2)}, u32[]{:S(2)}) async-start(f32[16,16,64,128]{3,1,2,0:T(8,128)} %copy.105), calls=%async_computation.3 | async-start | bytes 16777216 | tf_op jit(solution)/shard_map/all_to_all | solution.py:123
  187.0 222.0 %all-gather.2.cloned.1.call-start = ((), (), s32[]{:S(2)}) async-start(), calls=%async_computation.4 | async-start | bytes 9437184 | tf_op jit(solution)/shard_map/all_gather | solution.py:16
  326.4 4.9 %copy-start.2 = (bf16[32,8192]{1,0:T(8,128)(2,1)S(1)}, bf16[32,8192]{1,0:T(8,128)(2,1)}, u32[]{:S(2)}) copy-start(bf16[32,8192]{1,0:T(8,128)(2,1)} %param.9) | copy-start | bytes 1572868
  326.4 5.0 %copy-start.7 = (s32[32]{0:T(128)S(1)}, s32[32]{0:T(128)}, u32[]{:S(2)}) copy-start(s32[32]{0:T(128)} %param.11) | copy-start | bytes 388
  334.4 33.6 %copy-start.1 = (f32[32,8,8,32]{3,2,1,0:T(8,128)}, f32[32,8,8,32]{3,2,1,0:T(8,128)S(1)}, u32[]{:S(2)}) copy-start(f32[32,8,8,32]{3,2,1,0:T(8,128)S(1)} %get-tuple-element.229) | copy-start | bytes 786436
  360.6 13.9 %all-to-all-start.2 = ((f32[16,1,1024]{2,1,0:T(1,128)}), f32[16,1,1024]{2,1,0:T(1,128)S(1)}, u32[]{:S(2)}, u32[]{:S(2)}) async-start(f32[16,1,1024]{2,1,0:T(1,128)} %reshape.417), calls=%async_computation.2 | async-start | bytes 131072 | tf_op jit(solution)/shard_map/all_to_all | solution.py:120
  408.4 0.7 copy-start.4
  410.4 20.7 %copy-start.5 = (f32[32,64]{1,0:T(8,128)S(1)}, f32[32,64]{1,0:T(8,128)}, u32[]{:S(2)}) copy-start(f32[32,64]{1,0:T(8,128)} %copy.116) | copy-start | bytes 24580
  410.4 20.7 %copy-start.6 = (f32[32,64]{1,0:T(8,128)S(1)}, f32[32,64]{1,0:T(8,128)}, u32[]{:S(2)}) copy-start(f32[32,64]{1,0:T(8,128)} %copy.112) | copy-start | bytes 24580
Sparse Core Ops, SparseCore 0:
  331.4 55.9 all-gather.1
where the time goes:
time: 443 us; the launch traced here: 441 us
  waiting for transfers between devices  182 us (41%)
  matrix products  68 us (15%)
  local copies, waits for them, and re-layouts  60 us (14%)
  other arithmetic  53.4 us (12%)
  starting transfers between devices  32.3 us (7%)
  blocking collectives  32.2 us (7%)
  between operations  13.6 us (3%)
    all_to_all x1, waiting for transfers between devices, on_device(): lax.all_to_all(attended.reshape(sources, slot_count, H, HD), 'batch', spl...  122 us
    all_to_all x1, waiting for transfers between devices, on_device(): lax.all_to_all(outgoing, 'batch', split_axis=0, concat_axis=0, tiled=True)  55.8 us
    dot_general x1, matrix products, local_partial(): jnp.einsum('rkgd,pkd->rkgp', query_heads, key_heads, preferred_element_ty...  35.2 us
    all_gather x2, blocking collectives, combined_all(): gathered = jax.tree.map(lambda a: lax.all_gather(a, axis), part)  32.2 us
    dot_general x1, matrix products, local_partial(): jnp.einsum('rkgp,pkd->rkgd', weights.astype(jnp.bfloat16), value_heads, p...  27.6 us
    reduce_sum x1, other arithmetic, local_partial(): totals = jnp.sum(weights, axis=-1)  23.2 us
    add x8, other arithmetic, combine_parts(): earlier_part[2] * left_scale[..., None]  20.2 us
    unnamed x25, local copies, waits for them, and re-layouts  14.7 us
  transfers between devices with their start and end apart: 5, of which 3 were waited for; matrix products, arithmetic and copies ran while one was open for 17% of the time, Pallas kernels for 0%

commit v1 on v0

v1 whole, which is shorter than its diff:
```python
import jax
import jax.numpy as jnp
from jax import lax
from jax.experimental import pallas as pl
from jax.experimental.pallas import tpu as pltpu
from jax.sharding import PartitionSpec as P

H = 64
KVH = 8
HD = 128
G = H // KVH
SLOTS = 16
ROWS = 32
SLEN = 32
POS = 1024
HALF = KVH // 2
QCOLS = HALF * G * HD
NQ = 4 * G * SLOTS
NR = G * ROWS
STAT = 16
SCALE = 1.4426950408889634 / HD**0.5
MESH = pl.DeviceIdType.MESH
F32 = jnp.float32
BF16 = jnp.bfloat16


def dot(a, b, contract=((1,), (0,))):
    return lax.dot_general(a, b, (contract, ((), ())), preferred_element_type=F32)


def iota(shape, dim):
    return lax.broadcasted_iota(jnp.int32, shape, dim)


def in_three(value):
    high = value.astype(BF16).astype(F32)
    rest = value - high
    middle = rest.astype(BF16).astype(F32)
    return high, middle, rest - middle


def stat_rows(maxima, totals):
    width = maxima.shape[1]
    row = iota((STAT, width), 0)
    rows = jnp.zeros((STAT, width), F32)
    for place, value in enumerate(in_three(maxima) + in_three(totals)):
        rows = jnp.where(row == place, value, rows)
    return rows.astype(BF16)


def read_stats(rows):
    rows = rows.astype(F32)
    return rows[0:1] + rows[1:2] + rows[2:3], rows[3:4] + rows[4:5] + rows[5:6]


def merge(parts):
    top = parts[0][0]
    for part in parts[1:]:
        top = jnp.maximum(top, part[0])
    total, summed = 0.0, 0.0
    for maxima, totals, attended in parts:
        factor = jnp.exp2(maxima - top)
        total = total + totals * factor
        summed = summed + attended * factor
    return top, total, summed


def kernel(
    queries, docs, lengths, keys, values, suffix_keys, suffix_values, out,
    q_home, q_out, q_in, k_buf, v_buf, v_turned, sk_buf, sv_buf, s_out, s_stat,
    o_send, y_recv, x_send, h_recv, gathered,
    local_sem, kv_send, kv_recv, q_send, q_recv, y_ssem, y_rsem, x_ssem, x_rsem, g_ssem, g_rsem,
):
    ctx, batch = lax.axis_index("ctx"), lax.axis_index("batch")
    y, core = ctx // 2, ctx % 2
    x, z = batch // 4, batch % 4
    group = core * HALF + y

    def at_xz(dx, dz):
        return (ctx, ((x + dx) % 4) * 4 + (z + dz) % 4)

    def at_ctx(delta):
        return ((ctx + delta) % 8, batch)

    sibling = (y * 2 + (1 - core), batch)
    mine = pl.ds(pl.multiple_of(core * HALF * HD, HALF * HD), HALF * HD)
    theirs = pl.ds(pl.multiple_of((1 - core) * HALF * HD, HALF * HD), HALF * HD)
    group_cols = pl.ds(pl.multiple_of(group * HD, HD), HD)

    local = [
        pltpu.make_async_copy(
            queries.at[:, pl.ds(pl.multiple_of(core * QCOLS, QCOLS), QCOLS)], q_home, local_sem.at[0]
        ),
        pltpu.make_async_copy(keys.at[0, :, mine], k_buf.at[0], local_sem.at[1]),
        pltpu.make_async_copy(values.at[0, :, mine], v_buf.at[0], local_sem.at[2]),
        pltpu.make_async_copy(suffix_keys.at[:, :, group_cols], sk_buf, local_sem.at[3]),
        pltpu.make_async_copy(suffix_values.at[:, :, group_cols], sv_buf, local_sem.at[4]),
    ]
    for copy in local:
        copy.start()

    barrier = pltpu.get_barrier_semaphore()
    for dz in range(4):
        for dx in range(4):
            if dx or dz:
                pl.semaphore_signal(barrier, inc=1, device_id=at_xz(dx, dz), device_id_type=MESH)
    for delta in range(1, 8):
        pl.semaphore_signal(barrier, inc=1, device_id=at_ctx(delta), device_id_type=MESH)

    doc = jnp.bitwise_and(docs[...] - x + 4, 3)
    named = (iota((8, ROWS), 0) == doc).astype(F32)
    before = (iota((ROWS, ROWS), 0) < iota((ROWS, ROWS), 1)).astype(BF16)
    rank = jnp.sum(named * dot(named.astype(BF16), before), axis=0, keepdims=True)
    code = doc.astype(F32) * SLOTS + rank
    to_slots = (iota((4 * SLOTS, ROWS), 0).astype(F32) == code).astype(BF16)
    spread = (iota((ROWS, NR), 1) % ROWS == iota((ROWS, NR), 0)).astype(BF16)
    code_of = dot(jnp.broadcast_to(code, (8, ROWS)).astype(BF16), spread)[0:1]
    length_of = dot(jnp.broadcast_to(lengths[...], (8, ROWS)).astype(F32).astype(BF16), spread)[0:1]

    local[0].wait()
    for part in range(HALF):
        cols = slice(part * G * HD, (part + 1) * G * HD)
        slots = dot(to_slots, q_home[:, cols]).astype(BF16)
        for dx in range(4):
            q_out[dx, :, cols] = slots[dx * SLOTS : (dx + 1) * SLOTS]
    q_in[0, 0] = q_out[0]

    pl.semaphore_wait(barrier, 22)

    q_copies = {}
    for chunk in (0, 1, 2, 3):
        for place in range(4):
            if chunk or place:
                copy = pltpu.make_async_remote_copy(
                    src_ref=q_out.at[(4 - place) % 4],
                    dst_ref=q_in.at[chunk, place],
                    send_sem=q_send.at[chunk, place],
                    recv_sem=q_recv.at[chunk, place],
                    device_id=at_xz(4 - place, 4 - chunk),
                    device_id_type=MESH,
                )
                copy.start()
                q_copies[chunk, place] = copy
    kv_copies = [
        pltpu.make_async_remote_copy(
            src_ref=source.at[0, :, theirs],
            dst_ref=buffer.at[1],
            send_sem=kv_send.at[place],
            recv_sem=kv_recv.at[place],
            device_id=sibling,
            device_id_type=MESH,
        )
        for place, (source, buffer) in enumerate(((keys, k_buf), (values, v_buf)))
    ]
    for copy in kv_copies:
        copy.start()

    local[3].wait()
    local[4].wait()
    own = jnp.concatenate(
        [q_home[:, pl.ds(pl.multiple_of(y * G * HD + j * HD, HD), HD)] for j in range(G)], axis=0
    )
    scores = dot(sk_buf[...].reshape(ROWS * SLEN, HD), own, ((1,), (1,))) * SCALE
    row, col = iota((ROWS * SLEN, NR), 0), iota((ROWS * SLEN, NR), 1)
    live = (row // SLEN == col % ROWS) & ((row % SLEN).astype(F32) < length_of)
    scores = jnp.where(live, scores, -jnp.inf)
    top = jnp.max(scores, axis=0, keepdims=True)
    weights = jnp.where(live, jnp.exp2(scores - top), 0.0)
    s_stat[0:1] = top
    s_stat[1:2] = jnp.sum(weights, axis=0, keepdims=True)
    s_out[...] = dot(sv_buf[...].reshape(ROWS * SLEN, HD), weights.astype(BF16), ((0,), (0,)))

    def turn(source):
        def block(b, carry):
            rows = pl.ds(pl.multiple_of(b * 256, 256), 256)
            at = pl.ds(pl.multiple_of(source * POS + b * 256, 256), 256)
            v_turned[:, at] = jnp.transpose(v_buf[source, rows, :])
            return carry

        lax.fori_loop(0, POS // 256, block, 0)

    local[2].wait()
    turn(0)
    local[1].wait()
    kv_copies[0].wait_recv()
    kv_copies[1].wait_recv()
    turn(1)

    def attend(chunk):
        def head(h, carry):
            cols = pl.ds(pl.multiple_of(h * HD, HD), HD)
            q = jnp.concatenate(
                [
                    q_in[chunk, place, :, pl.ds(pl.multiple_of(h * G * HD + j * HD, HD), HD)]
                    for place in range(4)
                    for j in range(G)
                ],
                axis=0,
            )
            k = k_buf[:, :, cols].reshape(2 * POS, HD)
            scores = dot(k, q, ((1,), (1,)))
            top = jnp.max(scores, axis=0, keepdims=True) * SCALE
            weights = jnp.exp2(scores * SCALE - top)
            totals = jnp.sum(weights, axis=0, keepdims=True)
            attended = dot(v_turned[cols, :], weights.astype(BF16))
            o_send[chunk, h, 0:HD] = attended.astype(BF16)
            o_send[chunk, h, HD : HD + STAT] = stat_rows(top, totals)
            return carry

        lax.fori_loop(0, HALF, head, 0)

    y_copies, x_copies = {}, {}

    def send_y(chunk):
        for step in range(1, 4):
            copy = pltpu.make_async_remote_copy(
                src_ref=o_send.at[chunk, (y + step) % 4],
                dst_ref=y_recv.at[chunk, step - 1],
                send_sem=y_ssem.at[chunk, step - 1],
                recv_sem=y_rsem.at[chunk, step - 1],
                device_id=at_ctx(2 * step),
                device_id_type=MESH,
            )
            copy.start()
            y_copies[chunk, step] = copy

    def reduce_y(chunk):
        for step in range(1, 4):
            y_copies[chunk, step].wait_recv()

        def part(block):
            return read_stats(block[HD : HD + STAT]) + (block[0:HD].astype(F32),)

        parts = [part(o_send[chunk, y])] + [part(y_recv[chunk, i]) for i in range(3)]
        top, totals, attended = merge(parts)
        x_send[chunk, 0:HD] = attended.astype(BF16)
        x_send[chunk, HD : HD + STAT] = stat_rows(top, totals)
        for place in range(4):
            source = x_send.at[chunk, :, place * HD : (place + 1) * HD]
            back = (4 - place) % 4
            if chunk == 0 and place == 0:
                h_recv[0, :, 0:HD] = x_send[0, :, 0:HD]
                continue
            copy = pltpu.make_async_remote_copy(
                src_ref=source,
                dst_ref=h_recv.at[(4 - chunk) % 4, :, back * HD : (back + 1) * HD],
                send_sem=x_ssem.at[chunk, place],
                recv_sem=x_rsem.at[(4 - chunk) % 4, back],
                device_id=at_xz(place, chunk),
                device_id_type=MESH,
            )
            copy.start()
            x_copies[chunk, place] = copy

    for chunk in range(4):
        for place in range(4):
            if chunk or place:
                q_copies[chunk, place].wait_recv()
        attend(chunk)
        send_y(chunk)
        if chunk:
            reduce_y(chunk - 1)
    reduce_y(3)

    line = iota((NQ, NR), 0)
    place_of = (line // (G * SLOTS)) * SLOTS + line % SLOTS
    same_head = (line // SLOTS) % G == iota((NQ, NR), 1) // ROWS
    pick = (same_head & (place_of.astype(F32) == code_of)).astype(BF16)
    for copy in x_copies.values():
        copy.wait_recv()
    parts = [(s_stat[0:1], s_stat[1:2], s_out[...])]
    for source in range(4):
        rows = dot(h_recv[source], pick)
        parts.append(read_stats(rows[HD : HD + STAT]) + (rows[0:HD],))
    top, totals, attended = merge(parts)
    result = jnp.transpose(attended / totals).astype(BF16)
    block_cols = pl.ds(pl.multiple_of(group * G * HD, G * HD), G * HD)
    for j in range(G):
        gathered[:, pl.ds(pl.multiple_of(group * G * HD + j * HD, HD), HD)] = result[
            j * ROWS : (j + 1) * ROWS
        ]
    g_copies = []
    for delta in range(1, 8):
        copy = pltpu.make_async_remote_copy(
            src_ref=gathered.at[:, block_cols],
            dst_ref=gathered.at[:, block_cols],
            send_sem=g_ssem.at[delta - 1],
            recv_sem=g_rsem.at[delta - 1],
            device_id=at_ctx(delta),
            device_id_type=MESH,
        )
        copy.start()
        g_copies.append(copy)
    for delta in range(1, 8):
        source = (ctx + 8 - delta) % 8
        source_group = (source % 2) * HALF + source // 2
        source_cols = pl.ds(pl.multiple_of(source_group * G * HD, G * HD), G * HD)
        pltpu.make_async_remote_copy(
            src_ref=gathered.at[:, source_cols],
            dst_ref=gathered.at[:, source_cols],
            send_sem=g_ssem.at[delta - 1],
            recv_sem=g_rsem.at[delta - 1],
            device_id=at_ctx(delta),
            device_id_type=MESH,
        ).wait_recv()
    last = pltpu.make_async_copy(gathered, out, local_sem.at[5])
    last.start()
    for copies in (q_copies.values(), kv_copies, y_copies.values(), x_copies.values(), g_copies):
        for copy in copies:
            copy.wait_send()
    last.wait()


def on_device(queries, docs, lengths, keys, values, suffix_keys, suffix_values):
    anywhere = pl.BlockSpec(memory_space=pl.ANY)
    vmem = pl.BlockSpec(memory_space=pltpu.VMEM)
    dma = pltpu.SemaphoreType.DMA
    message = HD + STAT
    return pl.pallas_call(
        kernel,
        name="shared_prefix_attention",
        out_shape=jax.ShapeDtypeStruct((ROWS, H * HD), BF16),
        in_specs=[anywhere, vmem, vmem, anywhere, anywhere, anywhere, anywhere],
        out_specs=anywhere,
        scratch_shapes=[
            pltpu.VMEM((ROWS, QCOLS), BF16),
            pltpu.VMEM((4, SLOTS, QCOLS), BF16),
            pltpu.VMEM((4, 4, SLOTS, QCOLS), BF16),
            pltpu.VMEM((2, POS, HALF * HD), BF16),
            pltpu.VMEM((2, POS, HALF * HD), BF16),
            pltpu.VMEM((HALF * HD, 2 * POS), BF16),
            pltpu.VMEM((ROWS, SLEN, HD), BF16),
            pltpu.VMEM((ROWS, SLEN, HD), BF16),
            pltpu.VMEM((HD, NR), F32),
            pltpu.VMEM((8, NR), F32),
            pltpu.VMEM((4, HALF, message, NQ), BF16),
            pltpu.VMEM((4, 3, message, NQ), BF16),
            pltpu.VMEM((4, message, NQ), BF16),
            pltpu.VMEM((4, message, NQ), BF16),
            pltpu.VMEM((ROWS, H * HD), BF16),
            dma((6,)),
            dma((2,)),
            dma((2,)),
            dma((4, 4)),
            dma((4, 4)),
            dma((4, 3)),
            dma((4, 3)),
            dma((4, 4)),
            dma((4, 4)),
            dma((7,)),
            dma((7,)),
        ],
        compiler_params=pltpu.CompilerParams(
            collective_id=0, has_side_effects=True, vmem_limit_bytes=56 * 1024 * 1024
        ),
    )(
        queries, docs.reshape(1, ROWS), lengths.reshape(1, ROWS), keys, values, suffix_keys, suffix_values
    )


def solution(mesh):
    in_specs = (
        P("batch", None),
        P("batch", None),
        P("batch"),
        P("batch", "ctx", None),
        P("batch", "ctx", None),
        P("batch", None, None),
        P("batch", None, None),
    )
    return jax.shard_map(
        on_device, mesh=mesh, in_specs=in_specs, out_specs=P("batch", None), check_vma=False
    )
```

time: 443 us -> 74.6 us (0.17)
  waiting for transfers between devices: 182 us -> 0 us
  Pallas kernels: 0 us -> 72.6 us
  matrix products: 68 us -> 0 us
  local copies, waits for them, and re-layouts: 60 us -> 1.87 us
  other arithmetic: 53.4 us -> 0 us
  starting transfers between devices: 32.3 us -> 0 us
  blocking collectives: 32.2 us -> 0 us
  between operations: 13.6 us -> 0.01 us
    all_to_all x4 -> x0, waiting for transfers between devices: 182 us -> none  [the longest x1 122 us: on_device(): lax.all_to_all(attended.reshape(sources, slot_count, H, HD), 'batch', spl...]
    pallas_call x0 -> x1, Pallas kernels: none -> 72.6 us  [on_device(): pl.pallas_call(kernel, name='shared_prefix_attention', out_shape=jax.Shap...]
    dot_general x4 -> x0, matrix products: 68 us -> none  [the longest x1 35.2 us: local_partial(): jnp.einsum('rkgd,pkd->rkgp', query_heads, key_heads, preferred_element_ty...]
    all_to_all x4 -> x0, starting transfers between devices: 32.2 us -> none  [the longest x1 9.7 us: on_device(): lax.all_to_all(row_max.reshape(sources, slot_count, H), 'batch', split_ax...]
    all_gather x2 -> x0, blocking collectives: 32.2 us -> none  [combined_all(): gathered = jax.tree.map(lambda a: lax.all_gather(a, axis), part)]
    add x17 -> x0, other arithmetic: 25.5 us -> none  [the longest x8 20.2 us: combine_parts(): earlier_part[2] * left_scale[..., None]]
    reduce_sum x3 -> x0, other arithmetic: 24.7 us -> none  [the longest x1 23.2 us: local_partial(): totals = jnp.sum(weights, axis=-1)]
    unnamed x25 -> x1, local copies, waits for them, and re-layouts: 14.7 us -> 1.87 us
  transfers between devices with their start and end apart: 5 -> 0, of which waited for: 3 -> 0; matrix products, arithmetic and copies ran while one was open for 17% -> 0% of each run, Pallas kernels for 0% -> 0%
where the time goes in v1:
time: 74.6 us; the launch traced here: 74.5 us
  Pallas kernels  72.6 us (97%)
  local copies, waits for them, and re-layouts  1.87 us (3%)
    pallas_call x1, Pallas kernels, on_device(): pl.pallas_call(kernel, name='shared_prefix_attention', out_shape=jax.Shap...  72.6 us
    unnamed x1, local copies, waits for them, and re-layouts  1.87 us

profile of v1, /device:TPU:1, one launch (start us, length us, event | category | flops | bytes accessed | tf_op | source)
XLA Modules:
  0.0 74.5 jit_solution(3210762227251513235)
XLA Ops:
  0.0 72.6 %shared_prefix_attention.1 = bf16[32,8192]{1,0:T(8,128)(2,1)} custom-call(bf16[32,8192]{1,0:T(8,128)(2,1)} %queries.1, s32[1,32]{1,0:T(1,128)} %bitcast.2, s32[1,32]{1,0:T(1,128)} %bitcast.3, bf16[1,1024,1024]{2,1,0:T(8,128)(2,1)} %keys.1, bf16[1,1024,1024]{2,1,0:T(8,128)(2,1)} %values.1, bf16[32,32,1024]{2,1,0:T(8,128)(2,1)} %suffix_keys.1, ...), custom_call_target="tpu_custom_call" | custom-call | tf_op jit(solution)/shard_map/shared_prefix_attention/pallas_call | solution.py:319
  72.6 1.9 %copy.9 = bf16[32,8192]{1,0:T(8,128)(2,1)} copy(bf16[32,8192]{1,0:T(8,128)(2,1)} %shared_prefix_attention.1) | data formatting | bytes 1048576

commit v2 on v1

v2 whole, which is shorter than its diff:
```python
import jax
import jax.numpy as jnp
from jax import lax
from jax.experimental import pallas as pl
from jax.experimental.pallas import tpu as pltpu
from jax.sharding import PartitionSpec as P

H = 64
KVH = 8
HD = 128
G = H // KVH
SLOTS = 16
ROWS = 32
SLEN = 32
POS = 1024
HALF = KVH // 2
QCOLS = HALF * G * HD
NQ = 4 * G * SLOTS
NR = G * ROWS
STAT = 16
BLOCK = 512
ORDER = (2, 1, 3, 0)
SCALE = 1.4426950408889634 / HD**0.5
MESH = pl.DeviceIdType.MESH
F32 = jnp.float32
BF16 = jnp.bfloat16


def dot(a, b, contract=((1,), (0,))):
    return lax.dot_general(a, b, (contract, ((), ())), preferred_element_type=F32)


def iota(shape, dim):
    return lax.broadcasted_iota(jnp.int32, shape, dim)


def in_three(value):
    high = value.astype(BF16).astype(F32)
    rest = value - high
    middle = rest.astype(BF16).astype(F32)
    return high, middle, rest - middle


def stat_rows(maxima, totals):
    width = maxima.shape[1]
    row = iota((STAT, width), 0)
    rows = jnp.zeros((STAT, width), F32)
    for place, value in enumerate(in_three(maxima) + in_three(totals)):
        rows = jnp.where(row == place, value, rows)
    return rows.astype(BF16)


def read_stats(rows):
    rows = rows.astype(F32)
    return rows[0:1] + rows[1:2] + rows[2:3], rows[3:4] + rows[4:5] + rows[5:6]


def merge(parts):
    top = parts[0][0]
    for part in parts[1:]:
        top = jnp.maximum(top, part[0])
    total, summed = 0.0, 0.0
    for maxima, totals, attended in parts:
        factor = jnp.exp2(maxima - top)
        total = total + totals * factor
        summed = summed + attended * factor
    return top, total, summed


def kernel(
    queries, docs, lengths, keys, values, suffix_keys, suffix_values, out,
    q_home, q_out, q_relay, q_in, k_buf, v_buf, v_turned, sk_buf, sv_buf, s_out, s_stat, pick,
    scores_a, scores_b, o_send, y_relay, y_merged, y_recv, x_send, h_recv, gathered,
    local_sem, out_sem, kv_ssem, kv_rsem, qx_ssem, qx_rsem, qz_ssem, qz_rsem, qzz_ssem, qzz_rsem,
    y_ssem, y_rsem, x_ssem, x_rsem, g_ssem, g_rsem,
):
    ctx, batch = lax.axis_index("ctx"), lax.axis_index("batch")
    y, core = ctx // 2, ctx % 2
    x, z = batch // 4, batch % 4
    group = core * HALF + y

    def at_xz(dx, dz):
        return (ctx, ((x + dx) % 4) * 4 + (z + dz) % 4)

    def at_y(dy):
        return ((ctx + 2 * dy) % 8, batch)

    sibling = (y * 2 + (1 - core), batch)

    def cols(start, width):
        return pl.ds(pl.multiple_of(start * width, width), width)

    def heads(i):
        return (y + ORDER[i]) % 4

    sent = []

    def send(src, dst, send_sem, recv_sem, device):
        copy = pltpu.make_async_remote_copy(
            src_ref=src,
            dst_ref=dst,
            send_sem=send_sem,
            recv_sem=recv_sem,
            device_id=device,
            device_id_type=MESH,
        )
        copy.start()
        sent.append(copy)
        return copy

    barrier = pltpu.get_barrier_semaphore()
    for dz in range(4):
        for dx in range(4):
            if dx or dz:
                pl.semaphore_signal(barrier, inc=1, device_id=at_xz(dx, dz), device_id_type=MESH)
    for dy in range(1, 4):
        pl.semaphore_signal(barrier, inc=1, device_id=at_y(dy), device_id_type=MESH)
    pl.semaphore_signal(barrier, inc=1, device_id=sibling, device_id_type=MESH)

    local = [
        pltpu.make_async_copy(queries.at[:, cols(core, QCOLS)], q_home, local_sem.at[0]),
        pltpu.make_async_copy(keys.at[0, :, cols(core, HALF * HD)], k_buf.at[0], local_sem.at[1]),
        pltpu.make_async_copy(values.at[0, :, cols(core, HALF * HD)], v_buf.at[0], local_sem.at[2]),
        pltpu.make_async_copy(suffix_keys.at[:, :, cols(group, HD)], sk_buf, local_sem.at[3]),
        pltpu.make_async_copy(suffix_values.at[:, :, cols(group, HD)], sv_buf, local_sem.at[4]),
    ]
    for copy in local:
        copy.start()

    doc = jnp.bitwise_and(docs[...] - x + 4, 3)
    named = (iota((8, ROWS), 0) == doc).astype(F32)
    before = (iota((ROWS, ROWS), 0) < iota((ROWS, ROWS), 1)).astype(BF16)
    rank = jnp.sum(named * dot(named.astype(BF16), before), axis=0, keepdims=True)
    code = doc.astype(F32) * SLOTS + rank
    to_slots = (iota((4 * SLOTS, ROWS), 0).astype(F32) == code).astype(BF16)

    local[0].wait()
    for i in range(HALF):
        slots = dot(to_slots, q_home[:, cols(heads(i), G * HD)]).astype(BF16)
        q_in[0, i, 0] = slots[0:SLOTS]
        for dx in range(1, 4):
            q_out[dx - 1, i] = slots[dx * SLOTS : (dx + 1) * SLOTS]

    pl.semaphore_wait(barrier, 19)

    sides = ((0, 1), (1, 3))
    half = (slice(0, 2), slice(2, 4))
    relay, direct, forwarded, first_hop, second_hop = {}, {}, {}, {}, {}
    for i in range(HALF):
        relay[i] = send(
            q_out.at[1, i], q_relay.at[i], qx_ssem.at[i, 2], qx_rsem.at[i, 2], at_xz((1, 3)[i % 2], 0)
        )
        for side, step in sides:
            direct[i, side] = send(
                q_out.at[step - 1, i],
                q_in.at[0, i, 4 - step],
                qx_ssem.at[i, side],
                qx_rsem.at[i, side],
                at_xz(step, 0),
            )

    def x_forward(i):
        relay[i].wait_recv()
        forwarded[i] = send(
            q_relay.at[i], q_in.at[0, i, 2], qx_ssem.at[i, 3], qx_rsem.at[i, 3], at_xz((1, 3)[i % 2], 0)
        )

    def z_first(i):
        direct[i, 0].wait_recv()
        direct[i, 1].wait_recv()
        forwarded[i].wait_recv()
        for side, step in sides:
            first_hop[i, side] = send(
                q_in.at[0, i],
                q_in.at[4 - step, i],
                qz_ssem.at[i, side],
                qz_rsem.at[i, side],
                at_xz(0, step),
            )

    def z_second(i):
        for side, step in sides:
            first_hop[i, side].wait_recv()
            second_hop[i, side] = send(
                q_in.at[4 - step, i, half[side]],
                q_in.at[2, i, half[side]],
                qzz_ssem.at[i, side],
                qzz_rsem.at[i, side],
                at_xz(0, step),
            )

    def z_last(i):
        second_hop[i, 0].wait_recv()
        second_hop[i, 1].wait_recv()

    kv_copies = [
        send(source.at[0, :, cols(1 - core, HALF * HD)], buffer.at[1], kv_ssem.at[i], kv_rsem.at[i], sibling)
        for i, (source, buffer) in enumerate(((keys, k_buf), (values, v_buf)))
    ]

    spread = (iota((ROWS, NR), 1) % ROWS == iota((ROWS, NR), 0)).astype(BF16)
    code_of = dot(jnp.broadcast_to(code, (8, ROWS)).astype(BF16), spread)[0:1]
    length_of = dot(jnp.broadcast_to(lengths[...], (8, ROWS)).astype(F32).astype(BF16), spread)[0:1]
    local[3].wait()
    local[4].wait()
    own = jnp.concatenate([q_home[:, cols(y * G + j, HD)] for j in range(G)], axis=0)
    scores = dot(sk_buf[...].reshape(ROWS * SLEN, HD), own, ((1,), (1,))) * SCALE
    row, col = iota((ROWS * SLEN, NR), 0), iota((ROWS * SLEN, NR), 1)
    live = (row // SLEN == col % ROWS) & ((row % SLEN).astype(F32) < length_of)
    scores = jnp.where(live, scores, -jnp.inf)
    top = jnp.max(scores, axis=0, keepdims=True)
    weights = jnp.where(live, jnp.exp2(scores - top), 0.0)
    s_stat[0:1] = top
    s_stat[1:2] = jnp.sum(weights, axis=0, keepdims=True)
    s_out[...] = dot(sv_buf[...].reshape(ROWS * SLEN, HD), weights.astype(BF16), ((0,), (0,)))

    def turn(source):
        def block(b, carry):
            rows = cols(b, 256)
            v_turned[:, cols(source * (POS // 256) + b, 256)] = jnp.transpose(v_buf[source, rows, :])
            return carry

        lax.fori_loop(0, POS // 256, block, 0)

    x_forward(0)
    x_forward(1)
    local[2].wait()
    turn(0)
    z_first(0)
    x_forward(2)
    x_forward(3)
    local[1].wait()
    for copy in kv_copies:
        copy.wait_recv()
    turn(1)

    line = iota((NQ, NR), 0)
    place_of = (line // (G * SLOTS)) * SLOTS + line % SLOTS
    same_head = (line // SLOTS) % G == iota((NQ, NR), 1) // ROWS
    pick[...] = (same_head & (place_of.astype(F32) == code_of)).astype(BF16)

    def score_block(chunk, i, q, b, target, top):
        at = (b * BLOCK) % POS
        k = k_buf[b * BLOCK // POS, at : at + BLOCK, cols(heads(i), HD)]
        scores = dot(k, q, ((1,), (1,)))
        target[b * BLOCK : (b + 1) * BLOCK] = scores
        here = jnp.max(scores.reshape(BLOCK // 8, 8, NQ), axis=0)
        return here if top is None else jnp.maximum(top, here)

    def value_block(i, b, source, top, state):
        weights = jnp.exp2(source[b * BLOCK : (b + 1) * BLOCK] * SCALE - top)
        totals = jnp.sum(weights.reshape(BLOCK // 8, 8, NQ), axis=0)
        attended = dot(
            v_turned[cols(heads(i), HD), b * BLOCK : (b + 1) * BLOCK], weights.astype(BF16)
        )
        return (totals, attended) if state is None else (state[0] + totals, state[1] + attended)

    def unit(now, top, source, then, target):
        state, later = None, None
        if then is not None:
            chunk, i = then
            q = jnp.concatenate(
                [q_in[chunk, i, place, :, j * HD : (j + 1) * HD] for place in range(4) for j in range(G)],
                axis=0,
            )
        for b in range(2 * POS // BLOCK):
            if then is not None:
                later = score_block(*then, q, b, target, later)
            if now is not None:
                state = value_block(now[1], b, source, top, state)
        if now is not None:
            o_send[now[0], now[1], 0:HD] = state[1].astype(BF16)
            o_send[now[0], now[1], HD : HD + STAT] = stat_rows(
                top, jnp.sum(state[0], axis=0, keepdims=True)
            )
        if then is not None:
            return jnp.max(later, axis=0, keepdims=True) * SCALE

    def part(block):
        return read_stats(block[HD : HD + STAT]) + (block[0:HD].astype(F32),)

    def packed(target, state):
        top, totals, attended = state
        target[0:HD] = attended.astype(BF16)
        target[HD : HD + STAT] = stat_rows(top, totals)

    lanes = (slice(0, NQ // 2), slice(NQ // 2, NQ))
    y_waits, x_waits = {}, {}

    def after(chunk, i):
        if i == 0:
            for side, step in ((0, 1), (1, 3)):
                y_waits[chunk, side] = send(
                    o_send.at[chunk, 0, :, lanes[side]],
                    y_relay.at[chunk, side],
                    y_ssem.at[chunk, side],
                    y_rsem.at[chunk, side],
                    at_y(step),
                )
        elif i < 3:
            side, step = i - 1, (1, 3)[i - 1]
            y_waits[chunk, 2 + side] = send(
                o_send.at[chunk, i, :, lanes[1 - side]],
                y_recv.at[chunk, side, 0],
                y_ssem.at[chunk, 2 + side],
                y_rsem.at[chunk, 2 + side],
                at_y(step),
            )
            y_waits[chunk, side].wait_recv()
            packed(
                y_merged.at[chunk, side],
                merge([part(o_send[chunk, i, :, lanes[side]]), part(y_relay[chunk, side])]),
            )
            y_waits[chunk, 4 + side] = send(
                y_merged.at[chunk, side],
                y_recv.at[chunk, side, 1],
                y_ssem.at[chunk, 4 + side],
                y_rsem.at[chunk, 4 + side],
                at_y(step),
            )

    def to_home(chunk):
        for i in range(2, 6):
            y_waits[chunk, i].wait_recv()
        for side in range(2):
            state = merge(
                [
                    part(o_send[chunk, 3, :, lanes[side]]),
                    part(y_recv[chunk, side, 1]),
                    part(y_recv[chunk, 1 - side, 0]),
                ]
            )
            packed(x_send.at[chunk, :, lanes[side]], state)
        for place in range(4):
            back = (4 - place) % 4
            source = x_send.at[chunk, :, place * HD : (place + 1) * HD]
            if chunk == 0 and place == 0:
                h_recv[0, :, 0:HD] = x_send[0, :, 0:HD]
                continue
            x_waits[(4 - chunk) % 4, back] = send(
                source,
                h_recv.at[(4 - chunk) % 4, :, back * HD : (back + 1) * HD],
                x_ssem.at[chunk, place],
                x_rsem.at[(4 - chunk) % 4, back],
                at_xz(place, chunk),
            )

    units = (
        (0, 0), (0, 1), (0, 2), (1, 0), (3, 0), (1, 1), (1, 2), (2, 0),
        (3, 1), (3, 2), (2, 1), (2, 2), (1, 3), (3, 3), (2, 3), (0, 3),
    )
    before_unit = {
        0: [(z_first, 1)],
        1: [(z_first, 2)],
        2: [(z_second, 0), (z_first, 3)],
        4: [(z_second, 1)],
        5: [(z_second, 2)],
        6: [(z_last, 0)],
        8: [(z_second, 3)],
        9: [(z_last, 1)],
        10: [(z_last, 2)],
        13: [(z_last, 3)],
    }
    buffers = (scores_a, scores_b)
    top = unit(None, None, None, units[0], buffers[0])
    for n, now in enumerate(units):
        then = units[n + 1] if n + 1 < len(units) else None
        for step, i in before_unit.get(n, ()):
            step(i)
        top = unit(now, top, buffers[n % 2], then, buffers[(n + 1) % 2])
        after(*now)
        if now[1] == 3:
            to_home(now[0])

    parts = [(s_stat[0:1], s_stat[1:2], s_out[...])]
    for source in (3, 1, 2, 0):
        for back in range(4):
            if source or back:
                x_waits[source, back].wait_recv()
        rows = dot(h_recv[source], pick[...])
        parts.append(read_stats(rows[HD : HD + STAT]) + (rows[0:HD],))
    top, totals, attended = merge(parts)
    result = jnp.transpose(attended / totals).astype(BF16)
    for j in range(G):
        gathered[:, cols(group * G + j, HD)] = result[j * ROWS : (j + 1) * ROWS]

    def block_of(dy, side):
        at = side * HALF + (y + dy) % 4
        return gathered.at[:, cols(at, G * HD)]

    written = []

    def write(dy, side):
        at = side * HALF + (y + dy) % 4
        copy = pltpu.make_async_copy(
            block_of(dy, side), out.at[:, cols(at, G * HD)], out_sem.at[0 if side is core else 1, dy]
        )
        copy.start()
        written.append(copy)

    def arrived(dy, side, place, device):
        pltpu.make_async_remote_copy(
            src_ref=block_of(dy, side),
            dst_ref=block_of(dy, side),
            send_sem=g_ssem.at[place],
            recv_sem=g_rsem.at[place],
            device_id=device,
            device_id_type=MESH,
        ).wait_recv()

    for dy in (2, 1, 3):
        send(block_of(0, core), block_of(0, core), g_ssem.at[dy], g_rsem.at[dy], at_y(dy))
    send(block_of(0, core), block_of(0, core), g_ssem.at[0], g_rsem.at[0], sibling)
    write(0, core)
    for dy in (1, 3, 2):
        back = 4 - dy
        arrived(back, core, dy, at_y(dy))
        send(block_of(back, core), block_of(back, core), g_ssem.at[3 + dy], g_rsem.at[3 + dy], sibling)
        write(back, core)
    for dy in (0, 1, 3, 2):
        arrived((4 - dy) % 4, 1 - core, 3 + dy if dy else 0, sibling)
        write((4 - dy) % 4, 1 - core)
    for copy in sent:
        copy.wait_send()
    for copy in written:
        copy.wait()


def on_device(queries, docs, lengths, keys, values, suffix_keys, suffix_values):
    anywhere = pl.BlockSpec(memory_space=pl.ANY)
    vmem = pl.BlockSpec(memory_space=pltpu.VMEM)
    dma = pltpu.SemaphoreType.DMA
    message = HD + STAT
    return pl.pallas_call(
        kernel,
        name="shared_prefix_attention",
        out_shape=jax.ShapeDtypeStruct((ROWS, H * HD), BF16),
        in_specs=[anywhere, vmem, vmem, anywhere, anywhere, anywhere, anywhere],
        out_specs=anywhere,
        scratch_shapes=[
            pltpu.VMEM((ROWS, QCOLS), BF16),
            pltpu.VMEM((3, HALF, SLOTS, G * HD), BF16),
            pltpu.VMEM((HALF, SLOTS, G * HD), BF16),
            pltpu.VMEM((4, 4, HALF, SLOTS, G * HD), BF16),
            pltpu.VMEM((2, POS, HALF * HD), BF16),
            pltpu.VMEM((2, POS, HALF * HD), BF16),
            pltpu.VMEM((HALF * HD, 2 * POS), BF16),
            pltpu.VMEM((ROWS, SLEN, HD), BF16),
            pltpu.VMEM((ROWS, SLEN, HD), BF16),
            pltpu.VMEM((HD, NR), F32),
            pltpu.VMEM((8, NR), F32),
            pltpu.VMEM((NQ, NR), BF16),
            pltpu.VMEM((2 * POS, NQ), F32),
            pltpu.VMEM((2 * POS, NQ), F32),
            pltpu.VMEM((4, HALF, message, NQ), BF16),
            pltpu.VMEM((4, 2, message, NQ // 2), BF16),
            pltpu.VMEM((4, 2, message, NQ // 2), BF16),
            pltpu.VMEM((4, 2, 2, message, NQ // 2), BF16),
            pltpu.VMEM((4, message, NQ), BF16),
            pltpu.VMEM((4, message, NQ), BF16),
            pltpu.VMEM((ROWS, H * HD), BF16),
            dma((5,)),
            dma((2, 4)),
            dma((2,)),
            dma((2,)),
            dma((4, 4)),
            dma((4, 4)),
            dma((4, 2)),
            dma((4, 2)),
            dma((4, 2)),
            dma((4, 2)),
            dma((4, 6)),
            dma((4, 6)),
            dma((4, 4)),
            dma((4, 4)),
            dma((7,)),
            dma((7,)),
        ],
        compiler_params=pltpu.CompilerParams(
            collective_id=0, has_side_effects=True, vmem_limit_bytes=56 * 1024 * 1024
        ),
    )(
        queries, docs.reshape(1, ROWS), lengths.reshape(1, ROWS), keys, values, suffix_keys, suffix_values
    )


def solution(mesh):
    in_specs = (
        P("batch", None),
        P("batch", None),
        P("batch"),
        P("batch", "ctx", None),
        P("batch", "ctx", None),
        P("batch", None, None),
        P("batch", None, None),
    )
    return jax.shard_map(
        on_device, mesh=mesh, in_specs=in_specs, out_specs=P("batch", None), check_vma=False
    )
```

time: 74.6 us -> 58.9 us (0.79)
  Pallas kernels: 72.6 us -> 56.9 us
    pallas_call x1, Pallas kernels: 72.6 us -> 56.9 us  [on_device(): pl.pallas_call(kernel, name='shared_prefix_attention', out_shape=jax.Shap...]
where the time goes in v2:
time: 58.9 us; the launch traced here: 58.8 us
  Pallas kernels  56.9 us (97%)
  local copies, waits for them, and re-layouts  1.87 us (3%)
    pallas_call x1, Pallas kernels, on_device(): pl.pallas_call(kernel, name='shared_prefix_attention', out_shape=jax.Shap...  56.9 us
    unnamed x1, local copies, waits for them, and re-layouts  1.87 us

profile of v2, /device:TPU:1, one launch (start us, length us, event | category | flops | bytes accessed | tf_op | source)
XLA Modules:
  0.0 58.8 jit_solution(15311128971229078578)
XLA Ops:
  0.0 56.9 %shared_prefix_attention.1 = bf16[32,8192]{1,0:T(8,128)(2,1)} custom-call(bf16[32,8192]{1,0:T(8,128)(2,1)} %queries.1, s32[1,32]{1,0:T(1,128)} %bitcast.2, s32[1,32]{1,0:T(1,128)} %bitcast.3, bf16[1,1024,1024]{2,1,0:T(8,128)(2,1)} %keys.1, bf16[1,1024,1024]{2,1,0:T(8,128)(2,1)} %values.1, bf16[32,32,1024]{2,1,0:T(8,128)(2,1)} %suffix_keys.1, ...), custom_call_target="tpu_custom_call" | custom-call | tf_op jit(solution)/shard_map/shared_prefix_attention/pallas_call | solution.py:434
  56.9 1.9 %copy.9 = bf16[32,8192]{1,0:T(8,128)(2,1)} copy(bf16[32,8192]{1,0:T(8,128)(2,1)} %shared_prefix_attention.1) | data formatting | bytes 1048576

commit v3 on v2

--- a/solution.py
+++ b/solution.py
@@ -201,19 +201,6 @@
     spread = (iota((ROWS, NR), 1) % ROWS == iota((ROWS, NR), 0)).astype(BF16)
     code_of = dot(jnp.broadcast_to(code, (8, ROWS)).astype(BF16), spread)[0:1]
     length_of = dot(jnp.broadcast_to(lengths[...], (8, ROWS)).astype(F32).astype(BF16), spread)[0:1]
-    local[3].wait()
-    local[4].wait()
-    own = jnp.concatenate([q_home[:, cols(y * G + j, HD)] for j in range(G)], axis=0)
-    scores = dot(sk_buf[...].reshape(ROWS * SLEN, HD), own, ((1,), (1,))) * SCALE
-    row, col = iota((ROWS * SLEN, NR), 0), iota((ROWS * SLEN, NR), 1)
-    live = (row // SLEN == col % ROWS) & ((row % SLEN).astype(F32) < length_of)
-    scores = jnp.where(live, scores, -jnp.inf)
-    top = jnp.max(scores, axis=0, keepdims=True)
-    weights = jnp.where(live, jnp.exp2(scores - top), 0.0)
-    s_stat[0:1] = top
-    s_stat[1:2] = jnp.sum(weights, axis=0, keepdims=True)
-    s_out[...] = dot(sv_buf[...].reshape(ROWS * SLEN, HD), weights.astype(BF16), ((0,), (0,)))
-
     def turn(source):
         def block(b, carry):
             rows = cols(b, 256)
@@ -255,6 +242,8 @@
         )
         return (totals, attended) if state is None else (state[0] + totals, state[1] + attended)
 
+    lanes = (slice(0, NQ // 2), slice(NQ // 2, NQ))
+
     def unit(now, top, source, then, target):
         state, later = None, None
         if then is not None:
@@ -269,10 +258,11 @@
             if now is not None:
                 state = value_block(now[1], b, source, top, state)
         if now is not None:
-            o_send[now[0], now[1], 0:HD] = state[1].astype(BF16)
-            o_send[now[0], now[1], HD : HD + STAT] = stat_rows(
-                top, jnp.sum(state[0], axis=0, keepdims=True)
-            )
+            attended = state[1].astype(BF16)
+            stats = stat_rows(top, jnp.sum(state[0], axis=0, keepdims=True))
+            for side in range(2):
+                o_send[now[0], now[1], side, 0:HD] = attended[:, lanes[side]]
+                o_send[now[0], now[1], side, HD : HD + STAT] = stats[:, lanes[side]]
         if then is not None:
             return jnp.max(later, axis=0, keepdims=True) * SCALE
 
@@ -284,14 +274,13 @@
         target[0:HD] = attended.astype(BF16)
         target[HD : HD + STAT] = stat_rows(top, totals)
 
-    lanes = (slice(0, NQ // 2), slice(NQ // 2, NQ))
     y_waits, x_waits = {}, {}
 
     def after(chunk, i):
         if i == 0:
             for side, step in ((0, 1), (1, 3)):
                 y_waits[chunk, side] = send(
-                    o_send.at[chunk, 0, :, lanes[side]],
+                    o_send.at[chunk, 0, side],
                     y_relay.at[chunk, side],
                     y_ssem.at[chunk, side],
                     y_rsem.at[chunk, side],
@@ -300,7 +289,7 @@
         elif i < 3:
             side, step = i - 1, (1, 3)[i - 1]
             y_waits[chunk, 2 + side] = send(
-                o_send.at[chunk, i, :, lanes[1 - side]],
+                o_send.at[chunk, i, 1 - side],
                 y_recv.at[chunk, side, 0],
                 y_ssem.at[chunk, 2 + side],
                 y_rsem.at[chunk, 2 + side],
@@ -309,7 +298,7 @@
             y_waits[chunk, side].wait_recv()
             packed(
                 y_merged.at[chunk, side],
-                merge([part(o_send[chunk, i, :, lanes[side]]), part(y_relay[chunk, side])]),
+                merge([part(o_send[chunk, i, side]), part(y_relay[chunk, side])]),
             )
             y_waits[chunk, 4 + side] = send(
                 y_merged.at[chunk, side],
@@ -325,21 +314,24 @@
         for side in range(2):
             state = merge(
                 [
-                    part(o_send[chunk, 3, :, lanes[side]]),
+                    part(o_send[chunk, 3, side]),
                     part(y_recv[chunk, side, 1]),
                     part(y_recv[chunk, 1 - side, 0]),
                 ]
             )
-            packed(x_send.at[chunk, :, lanes[side]], state)
+            attended, stats = state[2].astype(BF16), stat_rows(state[0], state[1])
+            for place in range(2):
+                x_send[chunk, 2 * side + place, 0:HD] = attended[:, place * HD : (place + 1) * HD]
+                x_send[chunk, 2 * side + place, HD : HD + STAT] = stats[:, place * HD : (place + 1) * HD]
         for place in range(4):
             back = (4 - place) % 4
-            source = x_send.at[chunk, :, place * HD : (place + 1) * HD]
+            source = x_send.at[chunk, place]
             if chunk == 0 and place == 0:
-                h_recv[0, :, 0:HD] = x_send[0, :, 0:HD]
+                h_recv[0, 0] = x_send[0, 0]
                 continue
             x_waits[(4 - chunk) % 4, back] = send(
                 source,
-                h_recv.at[(4 - chunk) % 4, :, back * HD : (back + 1) * HD],
+                h_recv.at[(4 - chunk) % 4, back],
                 x_ssem.at[chunk, place],
                 x_rsem.at[(4 - chunk) % 4, back],
                 at_xz(place, chunk),
@@ -372,12 +364,25 @@
         if now[1] == 3:
             to_home(now[0])
 
+    local[3].wait()
+    local[4].wait()
+    own = jnp.concatenate([q_home[:, cols(y * G + j, HD)] for j in range(G)], axis=0)
+    scores = dot(sk_buf[...].reshape(ROWS * SLEN, HD), own, ((1,), (1,))) * SCALE
+    row, col = iota((ROWS * SLEN, NR), 0), iota((ROWS * SLEN, NR), 1)
+    live = (row // SLEN == col % ROWS) & ((row % SLEN).astype(F32) < length_of)
+    scores = jnp.where(live, scores, -jnp.inf)
+    top = jnp.max(scores, axis=0, keepdims=True)
+    weights = jnp.where(live, jnp.exp2(scores - top), 0.0)
+    s_stat[0:1] = top
+    s_stat[1:2] = jnp.sum(weights, axis=0, keepdims=True)
+    s_out[...] = dot(sv_buf[...].reshape(ROWS * SLEN, HD), weights.astype(BF16), ((0,), (0,)))
+
     parts = [(s_stat[0:1], s_stat[1:2], s_out[...])]
     for source in (3, 1, 2, 0):
         for back in range(4):
             if source or back:
                 x_waits[source, back].wait_recv()
-        rows = dot(h_recv[source], pick[...])
+        rows = dot(jnp.concatenate([h_recv[source, back] for back in range(4)], axis=1), pick[...])
         parts.append(read_stats(rows[HD : HD + STAT]) + (rows[0:HD],))
     top, totals, attended = merge(parts)
     result = jnp.transpose(attended / totals).astype(BF16)
@@ -452,12 +457,12 @@
             pltpu.VMEM((NQ, NR), BF16),
             pltpu.VMEM((2 * POS, NQ), F32),
             pltpu.VMEM((2 * POS, NQ), F32),
-            pltpu.VMEM((4, HALF, message, NQ), BF16),
+            pltpu.VMEM((4, HALF, 2, message, NQ // 2), BF16),
             pltpu.VMEM((4, 2, message, NQ // 2), BF16),
             pltpu.VMEM((4, 2, message, NQ // 2), BF16),
             pltpu.VMEM((4, 2, 2, message, NQ // 2), BF16),
-            pltpu.VMEM((4, message, NQ), BF16),
-            pltpu.VMEM((4, message, NQ), BF16),
+            pltpu.VMEM((4, 4, message, HD), BF16),
+            pltpu.VMEM((4, 4, message, HD), BF16),
             pltpu.VMEM((ROWS, H * HD), BF16),
             dma((5,)),
             dma((2, 4)),

time: 58.9 us -> 58.7 us (level)
  no operation moved by 1% of the time
where the time goes in v3:
time: 58.7 us; the launch traced here: 58.6 us
  Pallas kernels  56.7 us (97%)
  local copies, waits for them, and re-layouts  1.87 us (3%)
    pallas_call x1, Pallas kernels, on_device(): pl.pallas_call(kernel, name='shared_prefix_attention', out_shape=jax.Shap...  56.7 us
    unnamed x1, local copies, waits for them, and re-layouts  1.87 us

profile of v3, /device:TPU:1, one launch (start us, length us, event | category | flops | bytes accessed | tf_op | source)
XLA Modules:
  0.0 58.6 jit_solution(2775195510108689730)
XLA Ops:
  0.0 56.7 %shared_prefix_attention.1 = bf16[32,8192]{1,0:T(8,128)(2,1)} custom-call(bf16[32,8192]{1,0:T(8,128)(2,1)} %queries.1, s32[1,32]{1,0:T(1,128)} %bitcast.2, s32[1,32]{1,0:T(1,128)} %bitcast.3, bf16[1,1024,1024]{2,1,0:T(8,128)(2,1)} %keys.1, bf16[1,1024,1024]{2,1,0:T(8,128)(2,1)} %values.1, bf16[32,32,1024]{2,1,0:T(8,128)(2,1)} %suffix_keys.1, ...), custom_call_target="tpu_custom_call" | custom-call | tf_op jit(solution)/shard_map/shared_prefix_attention/pallas_call | solution.py:439
  56.7 1.9 %copy.9 = bf16[32,8192]{1,0:T(8,128)(2,1)} copy(bf16[32,8192]{1,0:T(8,128)(2,1)} %shared_prefix_attention.1) | data formatting | bytes 1048576
